TPU v7x, 512 devices: a whole 4x8x8 slice. The times are simulated.
512 devices in a mesh: tm: 16 (over y, core), height: 8 (over z), width: 4 (over x).
Axes of the slice: x: 4, y: 8, z: 8, core: 2. Of those that a mesh axis runs over, the one named last changes fastest.
Arguments:
- latents: bfloat16 [64, 64, 32, 512], P('tm', 'height', 'width'), may hold values from -6 to 6
- spatial_taps: float32 [3, 3, 512], replicated, may hold values from -2 to 2
- kernel_taps: bfloat16 [64, 512], replicated, may hold values from -0.4 to 0.4
- skip_gain: float32 [512], replicated, may hold values from 0.5 to 1.5
- gate_weight: bfloat16 [512, 512], replicated, may hold values from -0.25 to 0.25
- value_weight: bfloat16 [512, 512], replicated, may hold values from -0.25 to 0.25
- out_weight: bfloat16 [512, 512], replicated, may hold values from -0.25 to 0.25
Outputs:
- mixed_out: bfloat16 [64, 64, 32, 512], P('tm', 'height', 'width')
All inputs are finite; a program needn't handle non-finite values.
Results may differ from a plain program's by a relative error of at most 0.0064.
Values may be sent and summed in bfloat16 or wider, within the bound.
A program may use at most 64 MiB of HBM per device.

v0:
```python
import jax
import jax.numpy as jnp
from jax import lax
from jax.sharding import PartitionSpec as P


def with_halo(cells, sides, width):
    for axis, dim in sides:
        count = lax.axis_size(axis)
        ends = count - 1
        head = lax.slice_in_dim(cells, 0, width, axis=dim)
        tail = lax.slice_in_dim(cells, cells.shape[dim] - width, cells.shape[dim], axis=dim)
        cells = jnp.concatenate(
            [
                lax.ppermute(tail, axis, [(i, (i + 1) % count) for i in range(ends)]),
                cells,
                lax.ppermute(head, axis, [((i + 1) % count, i) for i in range(ends)]),
            ],
            axis=dim,
        )
    return cells


def spatial_mix(padded, spatial_taps):
    rows = padded.shape[1] - 2
    cols = padded.shape[2] - 2
    total = jnp.zeros((padded.shape[0], rows, cols, padded.shape[3]), jnp.float32)
    for first in range(3):
        for second in range(3):
            window = padded[:, first : first + rows, second : second + cols, :].astype(jnp.float32)
            total = total + window * spatial_taps[first, second]
    return total.astype(jnp.bfloat16)


def body(latents, spatial_taps, kernel_taps, skip_gain, gate_weight, value_weight, out_weight):
    frames_dev, rows, cols, chans = latents.shape
    clip_len = kernel_taps.shape[0]
    padded = with_halo(latents, (("height", 1), ("width", 2)), 1)
    spatial = spatial_mix(padded, spatial_taps)
    share = chans // lax.axis_size("tm")
    first = lax.axis_index("tm") * share
    local_taps = lax.dynamic_slice_in_dim(kernel_taps, first, share, 1)
    local_skip = lax.dynamic_slice_in_dim(skip_gain, first, share, 0)
    lag = (
        jnp.arange(clip_len, dtype=jnp.int32)[:, None]
        - jnp.arange(clip_len, dtype=jnp.int32)[None, :]
    )
    index = jnp.clip(lag, 0, clip_len - 1)
    picked = jnp.take(local_taps.T, index, axis=1)
    toeplitz = jnp.where(lag[None, :, :] >= 0, picked, jnp.zeros_like(picked))
    block = lax.all_to_all(spatial, "tm", split_axis=3, concat_axis=0, tiled=True)
    flat = block.reshape(clip_len, -1, share)
    causal = jnp.einsum("cts,sxc->txc", toeplitz, flat, preferred_element_type=jnp.float32)
    result = (causal + local_skip * flat.astype(jnp.float32)).astype(jnp.bfloat16)
    mixed = lax.all_to_all(
        result.reshape(block.shape), "tm", split_axis=0, concat_axis=3, tiled=True
    )
    flat_in = latents.reshape(-1, chans)
    flat_mixed = mixed.reshape(-1, chans)
    gate = jax.nn.silu(jnp.dot(flat_in, gate_weight, preferred_element_type=jnp.float32))
    value = jnp.dot(flat_mixed, value_weight, preferred_element_type=jnp.float32)
    hidden = (value * gate).astype(jnp.bfloat16)
    result = jnp.dot(hidden, out_weight, preferred_element_type=jnp.float32).astype(jnp.bfloat16)
    return result.reshape(latents.shape)


def solution(mesh):
    in_specs = (P("tm", "height", "width", None), P(), P(), P(), P(), P(), P())
    out_specs = P("tm", "height", "width", None)
    return jax.shard_map(body, mesh=mesh, in_specs=in_specs, out_specs=out_specs, check_vma=False)
```

profile of v0, /device:TPU:1, one launch (start us, length us, event | category | flops | bytes accessed | tf_op | source)
XLA Modules:
  0.0 100.3 jit_solution(6941042065050620593)
XLA Ops:
  0.0 0.8 fusion.29
  0.8 4.8 %collective-permute-start = (bf16[4,1,8,512]{3,2,1,0:T(8,128)(2,1)S(1)}, bf16[4,1,8,512]{3,2,1,0:T(8,128)(2,1)S(1)}, u32[]{:S(2)}, u32[]{:S(2)}) collective-permute-start(bf16[4,1,8,512]{3,2,1,0:T(8,128)(2,1)S(1)} %get-tuple-element.8), channel_id=1, source_target_pairs={{0,4},{4,8},{8,12},{12,16},{16,20},{20,24},{24,28},{1,5},{5,9},{9,... | collective-permute-start | bytes 98312 | tf_op jit(solution)/shard_map/ppermute | solution.py:15
  5.7 1.3 %collective-permute-start.1 = (bf16[4,1,8,512]{3,2,1,0:T(8,128)(2,1)S(1)}, bf16[4,1,8,512]{3,2,1,0:T(8,128)(2,1)S(1)}, u32[]{:S(2)}, u32[]{:S(2)}) collective-permute-start(bf16[4,1,8,512]{3,2,1,0:T(8,128)(2,1)S(1)} %get-tuple-element.7), channel_id=1, source_target_pairs={{4,0},{8,4},{12,8},{16,12},{20,16},{24,20},{28,24},{5,1},{9,5},{13... | collective-permute-start | bytes 98312 | tf_op jit(solution)/shard_map/ppermute | solution.py:17
  7.0 1.0 constant_dynamic-update-slice_fusion.1
  8.0 3.0 %collective-permute-done.1 = bf16[4,1,8,512]{3,2,1,0:T(8,128)(2,1)S(1)} collective-permute-done((bf16[4,1,8,512]{3,2,1,0:T(8,128)(2,1)S(1)}, bf16[4,1,8,512]{3,2,1,0:T(8,128)(2,1)S(1)}, u32[]{:S(2)}, u32[]{:S(2)}) %collective-permute-start.1) | collective-permute-done | bytes 32800 | tf_op jit(solution)/shard_map/ppermute | solution.py:17
  11.0 0.1 fusion.28
  11.1 3.1 %collective-permute-start.2 = (bf16[4,10,1,512]{3,1,2,0:T(8,128)(2,1)S(1)}, bf16[4,10,1,512]{3,1,2,0:T(8,128)(2,1)S(1)}, u32[]{:S(2)}, u32[]{:S(2)}) collective-permute-start(bf16[4,10,1,512]{3,1,2,0:T(8,128)(2,1)S(1)} %copy.96), channel_id=1, source_target_pairs={{0,1},{1,2},{2,3},{4,5},{5,6},{6,7},{8,9},{9,10},{10,11},{12,13},{... | collective-permute-start | bytes 122888 | tf_op jit(solution)/shard_map/ppermute | solution.py:15
  14.2 1.3 %collective-permute-start.3 = (bf16[4,10,1,512]{3,1,2,0:T(8,128)(2,1)S(1)}, bf16[4,10,1,512]{3,1,2,0:T(8,128)(2,1)S(1)}, u32[]{:S(2)}, u32[]{:S(2)}) collective-permute-start(bf16[4,10,1,512]{3,1,2,0:T(8,128)(2,1)S(1)} %copy.97), channel_id=1, source_target_pairs={{1,0},{2,1},{3,2},{5,4},{6,5},{7,6},{9,8},{10,9},{11,10},{13,12},{... | collective-permute-start | bytes 122888 | tf_op jit(solution)/shard_map/ppermute | solution.py:17
  15.5 0.9 fusion.30
  16.5 2.7 %collective-permute-done.3 = bf16[4,10,1,512]{3,1,2,0:T(8,128)(2,1)S(1)} collective-permute-done((bf16[4,10,1,512]{3,1,2,0:T(8,128)(2,1)S(1)}, bf16[4,10,1,512]{3,1,2,0:T(8,128)(2,1)S(1)}, u32[]{:S(2)}, u32[]{:S(2)}) %collective-permute-start.3) | collective-permute-done | bytes 40992 | tf_op jit(solution)/shard_map/ppermute | solution.py:17
  19.3 2.1 %add_convert_fusion = bf16[4,8,8,512]{3,2,1,0:T(8,128)(2,1)S(1)} fusion(bf16[4,8,8,512]{3,2,1,0:T(8,128)(2,1)} %param.7, bf16[4,10,8,512]{3,2,1,0:T(8,128)(2,1)S(1)} %constant_dynamic-update-slice_fusion, bf16[4,10,1,512]{3,2,1,0:T(2,128)(2,1)S(1)} %copy.88, bf16[4,10,1,512]{3,2,1,0:T(2,128)(2,1)S(1)} %copy.86, ...), kind=kLoop, calls=%fused_computation.24 | loop fusion | flops 6684672 | bytes 1017856 | tf_op jit(solution)/shard_map/convert_element_type | solution.py:32
  21.4 6.4 %copy.89 = bf16[4,8,8,512]{2,1,0,3:T(8,128)(2,1)} copy(bf16[4,8,8,512]{3,2,1,0:T(8,128)(2,1)S(1)} %add_convert_fusion) | data formatting | bytes 524288 | tf_op jit(solution)/shard_map/convert_element_type | solution.py:32
  27.8 6.4 %reshape.97 = bf16[16,2,4096]{2,1,0:T(2,128)(2,1)} reshape(bf16[512,4,8,8]{3,2,1,0:T(8,128)(2,1)} %bitcast.47) | data formatting | bytes 524288
  34.2 10.4 %all-to-all-start = ((bf16[16,2,4096]{2,1,0:T(2,128)(2,1)}), bf16[16,2,4096]{2,1,0:T(2,128)(2,1)S(1)}, u32[]{:S(2)}, u32[]{:S(2)}) async-start(bf16[16,2,4096]{2,1,0:T(2,128)(2,1)} %reshape.97), calls=%async_computation | async-start | bytes 524288 | tf_op jit(solution)/shard_map/all_to_all | solution.py:51
  44.6 0.1 reshape.90
  44.7 0.8 dynamic-slice_bitcast_fusion
  45.5 12.1 %gather_fusion = bf16[4096,32]{1,0:T(8,128)(2,1)S(1)} fusion(bf16[32,64]{0,1:T(8,128)(2,1)S(1)} %dynamic-slice_bitcast_fusion, s32[4096]{0:T(1024)S(1)} %broadcast_clamp_fusion), kind=kCustom, calls=%fused_computation | custom fusion | bytes 540672 | tf_op jit(solution)/shard_map/jit(_take)/gather | solution.py:49
  57.6 1.0 copy.91
  58.6 0.8 dynamic_slice.7
  59.4 6.0 %reshape.98 = bf16[512,4,8,8]{3,2,1,0:T(8,128)(2,1)} reshape(bf16[16,2,4096]{2,1,0:T(2,128)(2,1)S(1)} %all-to-all-done) | data formatting | bytes 524288
  65.3 5.3 %copy.90 = bf16[4,8,8,16,32]{4,2,1,0,3:T(8,128)(2,1)S(1)} copy(bf16[4,8,8,16,32]{2,1,0,4,3:T(8,128)(2,1)} %bitcast.46) | data formatting | bytes 524288 | tf_op jit(solution)/shard_map/all_to_all | solution.py:51
  70.7 1.6 %copy.92 = bf16[64,64,32]{0,1,2:T(8,128)(2,1)S(1)} copy(bf16[64,64,32]{2,1,0:T(8,128)(2,1)S(1)} %bitcast.48) | data formatting | bytes 524288 | tf_op jit(solution)/shard_map/reshape | solution.py:52
  72.3 0.4 fusion.2
  72.8 1.7 %copy.94 = bf16[64,8,8,32]{3,2,1,0:T(8,128)(2,1)S(1)} copy(bf16[64,8,8,32]{0,2,1,3:T(8,128)(2,1)S(1)} %fusion.2) | data formatting | bytes 524288 | tf_op jit(solution)/shard_map/reshape | solution.py:56
  74.5 1.7 %reshape.99 = bf16[16,2,4096]{2,1,0:T(2,128)(2,1)} reshape(bf16[64,8,8,32]{3,2,1,0:T(8,128)(2,1)S(1)} %copy.94) | data formatting | bytes 524288
  76.2 7.2 %all-to-all-start.1 = ((bf16[16,2,4096]{2,1,0:T(2,128)(2,1)}), bf16[16,2,4096]{2,1,0:T(2,128)(2,1)S(1)}, u32[]{:S(2)}, u32[]{:S(2)}) async-start(bf16[16,2,4096]{2,1,0:T(2,128)(2,1)} %reshape.99), calls=%async_computation.1 | async-start | bytes 524288 | tf_op jit(solution)/shard_map/all_to_all | solution.py:55
  83.4 0.3 fusion.31
  83.7 11.4 %all-to-all-done.1 = bf16[16,2,4096]{2,1,0:T(2,128)(2,1)S(1)} async-done(((bf16[16,2,4096]{2,1,0:T(2,128)(2,1)}), bf16[16,2,4096]{2,1,0:T(2,128)(2,1)S(1)}, u32[]{:S(2)}, u32[]{:S(2)}) %all-to-all-start.1) | async-done | bytes 262176 | tf_op jit(solution)/shard_map/all_to_all | solution.py:55
  95.1 0.5 reshape.100
  95.6 1.2 %copy.95 = bf16[4,8,8,16,32]{4,3,2,1,0:T(8,128)(2,1)S(1)} copy(bf16[4,8,8,16,32]{4,2,1,0,3:T(8,128)(2,1)S(1)} %bitcast.49) | data formatting | bytes 524288 | tf_op jit(solution)/shard_map/all_to_all | solution.py:55
  96.8 1.0 reshape.85
  97.8 2.4 %convolution_convert_fusion = bf16[256,512]{1,0:T(8,128)(2,1)} fusion(bf16[512,512]{1,0:T(8,128)(2,1)} %param.13, bf16[256,512]{1,0:T(8,128)(2,1)S(1)} %reshape.85, bf16[512,512]{1,0:T(8,128)(2,1)} %param.12, f32[256,512]{1,0:T(8,128)S(1)} %fusion.31), kind=kOutput, calls=%fused_computation.7 | convolution fusion | flops 269352960 | bytes 2097152 | tf_op jit(solution)/shard_map/dot_general | solution.py:63
  (16 shorter events, 0.2 us)
Async XLA Ops:
  0.0 83.4 %copy-start = (bf16[512,512]{1,0:T(8,128)(2,1)S(1)}, bf16[512,512]{1,0:T(8,128)(2,1)}, u32[]{:S(2)}) copy-start(bf16[512,512]{1,0:T(8,128)(2,1)} %param.11) | copy-start | bytes 1572868
  0.8 6.1 %collective-permute-start = (bf16[4,1,8,512]{3,2,1,0:T(8,128)(2,1)S(1)}, bf16[4,1,8,512]{3,2,1,0:T(8,128)(2,1)S(1)}, u32[]{:S(2)}, u32[]{:S(2)}) collective-permute-start(bf16[4,1,8,512]{3,2,1,0:T(8,128)(2,1)S(1)} %get-tuple-element.8), channel_id=1, source_target_pairs={{0,4},{4,8},{8,12},{12,16},{16,20},{20,24},{24,28},{1,5},{5,9},{9,... | collective-permute-start | bytes 98312 | tf_op jit(solution)/shard_map/ppermute | solution.py:15
  5.7 5.3 %collective-permute-start.1 = (bf16[4,1,8,512]{3,2,1,0:T(8,128)(2,1)S(1)}, bf16[4,1,8,512]{3,2,1,0:T(8,128)(2,1)S(1)}, u32[]{:S(2)}, u32[]{:S(2)}) collective-permute-start(bf16[4,1,8,512]{3,2,1,0:T(8,128)(2,1)S(1)} %get-tuple-element.7), channel_id=1, source_target_pairs={{4,0},{8,4},{12,8},{16,12},{20,16},{24,20},{28,24},{5,1},{9,5},{13... | collective-permute-start | bytes 98312 | tf_op jit(solution)/shard_map/ppermute | solution.py:17
  11.1 5.3 %collective-permute-start.2 = (bf16[4,10,1,512]{3,1,2,0:T(8,128)(2,1)S(1)}, bf16[4,10,1,512]{3,1,2,0:T(8,128)(2,1)S(1)}, u32[]{:S(2)}, u32[]{:S(2)}) collective-permute-start(bf16[4,10,1,512]{3,1,2,0:T(8,128)(2,1)S(1)} %copy.96), channel_id=1, source_target_pairs={{0,1},{1,2},{2,3},{4,5},{5,6},{6,7},{8,9},{9,10},{10,11},{12,13},{... | collective-permute-start | bytes 122888 | tf_op jit(solution)/shard_map/ppermute | solution.py:15
  14.2 5.0 %collective-permute-start.3 = (bf16[4,10,1,512]{3,1,2,0:T(8,128)(2,1)S(1)}, bf16[4,10,1,512]{3,1,2,0:T(8,128)(2,1)S(1)}, u32[]{:S(2)}, u32[]{:S(2)}) collective-permute-start(bf16[4,10,1,512]{3,1,2,0:T(8,128)(2,1)S(1)} %copy.97), channel_id=1, source_target_pairs={{1,0},{2,1},{3,2},{5,4},{6,5},{7,6},{9,8},{10,9},{11,10},{13,12},{... | collective-permute-start | bytes 122888 | tf_op jit(solution)/shard_map/ppermute | solution.py:17
  34.2 25.1 %all-to-all-start = ((bf16[16,2,4096]{2,1,0:T(2,128)(2,1)}), bf16[16,2,4096]{2,1,0:T(2,128)(2,1)S(1)}, u32[]{:S(2)}, u32[]{:S(2)}) async-start(bf16[16,2,4096]{2,1,0:T(2,128)(2,1)} %reshape.97), calls=%async_computation | async-start | bytes 524288 | tf_op jit(solution)/shard_map/all_to_all | solution.py:51
  70.7 12.7 %copy-start.1 = (bf16[4,8,8,512]{3,2,1,0:T(8,128)(2,1)S(1)}, bf16[4,8,8,512]{3,2,1,0:T(8,128)(2,1)}, u32[]{:S(2)}) copy-start(bf16[4,8,8,512]{3,2,1,0:T(8,128)(2,1)} %param.7) | copy-start | bytes 786436
  76.2 18.9 %all-to-all-start.1 = ((bf16[16,2,4096]{2,1,0:T(2,128)(2,1)}), bf16[16,2,4096]{2,1,0:T(2,128)(2,1)S(1)}, u32[]{:S(2)}, u32[]{:S(2)}) async-start(bf16[16,2,4096]{2,1,0:T(2,128)(2,1)} %reshape.99), calls=%async_computation.1 | async-start | bytes 524288 | tf_op jit(solution)/shard_map/all_to_all | solution.py:55
where the time goes:
time: 102 us; the launch traced here: 100 us
  local copies, waits for them, and re-layouts  49.5 us (49%)
  starting transfers between devices  28.1 us (28%)
  waiting for transfers between devices  17.2 us (17%)
  matrix products  3.13 us (3%)
  other arithmetic  2.15 us (2%)
    unnamed x12, local copies, waits for them, and re-layouts  15.6 us
    gather x2, local copies, waits for them, and re-layouts, body(): picked = jnp.take(local_taps.T, index, axis=1)  13.1 us
    all_to_all x1, waiting for transfers between devices, body(): lax.all_to_all(result.reshape(block.shape), 'tm', split_axis=0, concat_ax...  11.4 us
    all_to_all x1, starting transfers between devices, body(): lax.all_to_all(spatial, 'tm', split_axis=3, concat_axis=0, tiled=True)  10.4 us
    ppermute x2, starting transfers between devices, with_halo(): lax.ppermute(tail, axis, [(i, (i + 1) % count) for i in range(ends)])  7.93 us
    all_to_all x1, starting transfers between devices, body(): lax.all_to_all(result.reshape(block.shape), 'tm', split_axis=0, concat_ax...  7.23 us
    convert_element_type x1, local copies, waits for them, and re-layouts, spatial_mix(): return total.astype(jnp.bfloat16)  6.37 us
    ppermute x2, waiting for transfers between devices, with_halo(): lax.ppermute(head, axis, [((i + 1) % count, i) for i in range(ends)])  5.75 us
  transfers between devices with their start and end apart: 6, of which 3 were waited for; matrix products, arithmetic and copies ran while one was open for 17% of the time, Pallas kernels for 0%

commit v1 on v0

v1 whole, which is shorter than its diff:
```python
import functools

import jax
import jax.numpy as jnp
from jax import lax
from jax.experimental import pallas as pl
from jax.experimental.pallas import tpu as pltpu
from jax.sharding import PartitionSpec as P

MESH = pl.DeviceIdType.MESH
F32 = jnp.float32
BF16 = jnp.bfloat16
ORDER = (1, 7, 2, 6, 3, 5, 4, 0)
AROUND = ((-1, 0), (1, 0), (0, -1), (0, 1), (-1, -1), (-1, 1), (1, -1), (1, 1))


def owner(group, tile):
    return ((group % 2) * 4 + tile) * 2 + group // 2


def kernel(
    lat, taps, ktaps, skip, wg, wv, hid,
    xl, tv, kt, kf, kb, sk, wgv, wvv, s0, s1, colb, crnb, hrow, hcol, hcrn, hc32, hk32,
    sendb, xin, retb, mixin, gate,
    lsem, hs, hr, fs, fr, rs, rr,
):
    me = lax.axis_index("tm")
    ring, core = me // 2, lax.rem(me, 2)
    hi, wi = lax.axis_index("height"), lax.axis_index("width")
    nh, nw = lax.axis_size("height"), lax.axis_size("width")
    mine = lax.rem(ring, 4)
    lanes = pl.ds(pl.multiple_of(mine * 128, 128), 128)

    loads = [
        pltpu.make_async_copy(lat, xl, lsem.at[0]),
        pltpu.make_async_copy(taps, tv, lsem.at[1]),
        pltpu.make_async_copy(ktaps.at[:, lanes], kt, lsem.at[2]),
        pltpu.make_async_copy(skip.at[:, lanes], sk, lsem.at[3]),
        pltpu.make_async_copy(wg, wgv, lsem.at[4]),
        pltpu.make_async_copy(wv, wvv, lsem.at[5]),
    ]
    loads[0].start()
    loads[1].start()

    def peer(index):
        return (index, hi, wi)

    def beside(step):
        dh, dw = step
        return (me, lax.rem(hi + dh + nh, nh), lax.rem(wi + dw + nw, nw))

    barrier = pltpu.get_barrier_semaphore()
    for step in range(1, 16):
        pl.semaphore_signal(barrier, inc=1, device_id=peer(lax.rem(me + step, 16)), device_id_type=MESH)
    for step in AROUND:
        pl.semaphore_signal(barrier, inc=1, device_id=beside(step), device_id_type=MESH)
    for load in loads[2:]:
        load.start()

    loads[0].wait()
    for tile in range(4):
        for frame in range(4):
            at = (tile * 4 + frame) * 64
            s0[at : at + 64] = xl[frame, :, :, tile * 128 : tile * 128 + 128].astype(F32).reshape(64, 128)
    colb[0] = s0[pl.ds(0, 128, stride=8)].astype(BF16)
    colb[1] = s0[pl.ds(7, 128, stride=8)].astype(BF16)
    for n, site in enumerate((0, 7, 56, 63)):
        crnb[n] = s0[pl.ds(site, 16, stride=64)].astype(BF16)

    pl.semaphore_wait(barrier, 23)

    pieces = (
        (xl.at[:, 0], hrow.at[1]),
        (xl.at[:, 7], hrow.at[0]),
        (colb.at[0], hcol.at[1]),
        (colb.at[1], hcol.at[0]),
        (crnb.at[0], hcrn.at[3]),
        (crnb.at[1], hcrn.at[2]),
        (crnb.at[2], hcrn.at[1]),
        (crnb.at[3], hcrn.at[0]),
    )
    opposite = (1, 0, 3, 2, 7, 6, 5, 4)
    halo = []
    for n, (src, dst) in enumerate(pieces):
        halo.append(
            pltpu.make_async_remote_copy(
                src_ref=src, dst_ref=dst, send_sem=hs.at[n], recv_sem=hr.at[opposite[n]],
                device_id=beside(AROUND[n]), device_id_type=MESH,
            )
        )
    for copy in halo:
        copy.start()

    sub = lax.broadcasted_iota(jnp.int32, (8, 128), 0)
    first, last = sub == 0, sub == 7
    edge = first | last

    def tap(tile, a, b):
        return tv[a, pl.ds(b, 1), pl.ds(pl.multiple_of(tile * 128, 128), 128)]

    def west(x):
        return jnp.where(first, 0.0, pltpu.roll(x, 1, 0))

    def east(x):
        return jnp.where(last, 0.0, pltpu.roll(x, 7, 0))

    loads[1].wait()

    def inside(i, carry):
        tile, frame = i // 4, lax.rem(i, 4)
        base = pl.multiple_of(i * 64, 64)
        weights = [[tap(tile, a, b) for b in range(3)] for a in range(3)]
        total = [None] * 8
        for r in range(8):
            x = s0[pl.ds(base + r * 8, 8)]
            moved = (west(x), x, east(x))
            for a in range(3):
                o = r + 1 - a
                if 0 <= o < 8:
                    part = weights[a][0] * moved[0] + weights[a][1] * moved[1] + weights[a][2] * moved[2]
                    total[o] = part if total[o] is None else total[o] + part
        for r in (0, 5, 6, 7):
            s1[pl.ds(base + r * 8, 8)] = total[r]
        for r in (1, 2, 3, 4):
            s1[pl.ds(base + r * 8, 8)] = total[r]
        mixed = [
            jnp.where(edge, pltpu.roll(total[5], 6, 0), total[1]),
            jnp.where(edge, pltpu.roll(total[5], 4, 0), total[2]),
            jnp.where(edge, pltpu.roll(total[5], 2, 0), total[3]),
            jnp.where(edge, pltpu.roll(total[6], 6, 0), total[4]),
        ]
        sendb[tile * 2, frame] = jnp.concatenate(mixed[:2], 0).astype(BF16)
        sendb[(4 + tile) * 2, frame] = jnp.concatenate(mixed[2:], 0).astype(BF16)
        return carry

    lax.fori_loop(0, 16, inside, 0)

    def forward(dest):
        return pltpu.make_async_remote_copy(
            src_ref=sendb.at[dest], dst_ref=xin.at[me], send_sem=fs.at[dest], recv_sem=fr.at[me],
            device_id=peer(dest), device_id_type=MESH,
        )

    def keep():
        return pltpu.make_async_copy(sendb.at[me], xin.at[me], fr.at[me])

    def spread(which):
        for step in ORDER:
            dest = lax.rem(ring + step, 8) * 2 + which
            if step:
                forward(dest).start()
            else:
                @pl.when(core == which)
                def _():
                    keep().start()

                @pl.when(core != which)
                def _():
                    forward(dest).start()

    spread(0)

    for n, (src, dst) in enumerate(pieces):
        pltpu.make_async_remote_copy(
            src_ref=src, dst_ref=(hrow.at[0], hrow.at[1], hcol.at[0], hcol.at[1], hcrn.at[0], hcrn.at[1], hcrn.at[2], hcrn.at[3])[n],
            send_sem=hs.at[n], recv_sem=hr.at[n], device_id=beside(AROUND[n]), device_id_type=MESH,
        ).wait_recv()

    up = (hi > 0).astype(F32)
    down = (hi < nh - 1).astype(F32)
    left = (wi > 0).astype(F32)
    right = (wi < nw - 1).astype(F32)
    hk32[0] = hcol[0].astype(F32) * left
    hk32[1] = hcol[1].astype(F32) * right
    hc32[0] = hcrn[0].astype(F32) * (up * left)
    hc32[1] = hcrn[1].astype(F32) * (up * right)
    hc32[2] = hcrn[2].astype(F32) * (down * left)
    hc32[3] = hcrn[3].astype(F32) * (down * right)

    def border(i, carry):
        tile, frame = i // 4, lax.rem(i, 4)
        base = pl.multiple_of(i * 64, 64)
        chans = pl.ds(pl.multiple_of(tile * 128, 128), 128)
        weights = [[tap(tile, a, b) for b in range(3)] for a in range(3)]
        above = hrow[0, frame, :, chans].astype(F32) * up
        below = hrow[1, frame, :, chans].astype(F32) * down
        row0 = s1[pl.ds(base, 8)] + (weights[0][0] * west(above) + weights[0][1] * above + weights[0][2] * east(above))
        row7 = s1[pl.ds(base + 56, 8)] + (weights[2][0] * west(below) + weights[2][1] * below + weights[2][2] * east(below))
        row6 = s1[pl.ds(base + 48, 8)]
        s1[pl.ds(base, 8)] = row0
        s1[pl.ds(base + 56, 8)] = row7
        ends = [
            jnp.where(edge, pltpu.roll(row6, 4, 0), row0),
            jnp.where(edge, pltpu.roll(row6, 2, 0), row7),
        ]
        sides = []
        for n, c in ((0, 0), (1, 7)):
            own = s1[pl.ds(base + c, 8, stride=8)]
            out = hk32[n, pl.ds(pl.multiple_of(i * 8, 8), 8)]
            over = jnp.where(first, hc32[n, pl.ds(i, 1)], pltpu.roll(out, 1, 0))
            under = jnp.where(last, hc32[2 + n, pl.ds(i, 1)], pltpu.roll(out, 7, 0))
            b = 2 * n
            sides.append(own + (weights[0][b] * over + weights[1][b] * out + weights[2][b] * under))
        sendb[tile * 2 + 1, frame] = jnp.concatenate(sides, 0).astype(BF16)
        sendb[(4 + tile) * 2 + 1, frame] = jnp.concatenate(ends, 0).astype(BF16)
        return carry

    lax.fori_loop(0, 16, border, 0)
    spread(1)

    loads[2].wait()
    loads[3].wait()
    kf[...] = kt[...].astype(F32)
    kb[0:8] = jnp.zeros((8, 8, 128), F32)

    def widen(lag, carry):
        kb[8 + lag] = jnp.broadcast_to(kf[pl.ds(lag, 1)], (8, 128))
        return carry

    lax.fori_loop(0, 64, widen, 0)
    kb[8] = kb[8] + jnp.broadcast_to(sk[...], (8, 128))
    loads[4].wait()
    raw = jnp.dot(xl[...].reshape(256, 512), wgv[...], preferred_element_type=F32)
    gate[...] = raw / (1.0 + jnp.exp(-raw))
    loads[5].wait()

    keep().wait()
    for step in range(1, 16):
        src = lax.rem(me + step, 16)
        pltpu.make_async_remote_copy(
            src_ref=sendb.at[src], dst_ref=xin.at[src], send_sem=fs.at[src], recv_sem=fr.at[src],
            device_id=peer(src), device_id_type=MESH,
        ).wait_recv()

    def back(dest):
        return pltpu.make_async_remote_copy(
            src_ref=retb.at[dest], dst_ref=mixin.at[me], send_sem=rs.at[dest], recv_sem=rr.at[me],
            device_id=peer(dest), device_id_type=MESH,
        )

    def own():
        return pltpu.make_async_copy(retb.at[me], mixin.at[me], rr.at[me])

    for step in ORDER:
        chip = lax.rem(ring + step, 8)

        def lagged(source, acc):
            shift = 8 + 8 * (chip - source)
            for s in range(8):
                x = xin[source * 2 + s // 4, s % 4].astype(F32).reshape(1, 2, 8, 128)
                acc = acc + kb[pl.ds(shift - s, 8)].reshape(8, 1, 8, 128) * x
            return acc

        acc = lax.fori_loop(0, chip + 1, lagged, jnp.zeros((8, 2, 8, 128), F32))
        retb[pl.ds(chip * 2, 2)] = acc.reshape(2, 4, 16, 128).astype(BF16)
        if step:
            back(chip * 2).start()
            back(chip * 2 + 1).start()
        else:
            own().start()
            back(chip * 2 + 1 - core).start()

    def arrived(which):
        for step in ORDER:
            src = lax.rem(ring + step, 8) * 2 + which

            def wait():
                pltpu.make_async_remote_copy(
                    src_ref=retb.at[src], dst_ref=mixin.at[src], send_sem=rs.at[src], recv_sem=rr.at[src],
                    device_id=peer(src), device_id_type=MESH,
                ).wait_recv()

            if step:
                wait()
            else:
                pl.when(core == which)(lambda: own().wait())
                pl.when(core != which)(wait)

    def values(which):
        rows = []
        for group in (2 * which, 2 * which + 1):
            rows.append(jnp.concatenate([mixin[owner(group, t)].reshape(64, 128) for t in range(4)], 1))
        return jnp.dot(jnp.concatenate(rows, 0), wvv[...], preferred_element_type=F32)

    def part(block, group, tile, frame, half):
        at = group * 64 + frame * 16 + half * 8
        return block[at : at + 8, tile * 128 : tile * 128 + 128]

    arrived(0)
    v = values(0)
    for tile in range(4):
        for frame in range(4):
            base = (tile * 4 + frame) * 64
            one, two = part(v, 0, tile, frame, 0), part(v, 0, tile, frame, 1)
            three, four = part(v, 1, tile, frame, 0), part(v, 1, tile, frame, 1)
            s1[base + 8 : base + 16] = one
            s1[base + 16 : base + 24] = two
            s1[base + 24 : base + 32] = three
            s1[base + 32 : base + 40] = four
            s1[base + 40 : base + 48] = jnp.where(
                sub < 3, pltpu.roll(one, 2, 0), jnp.where(sub < 5, pltpu.roll(two, 4, 0), pltpu.roll(three, 6, 0))
            )
            s1[base + 48 : base + 56] = pltpu.roll(four, 2, 0)
    arrived(1)
    v = values(1)
    for tile in range(4):
        for frame in range(4):
            base = (tile * 4 + frame) * 64
            top, bottom = part(v, 1, tile, frame, 0), part(v, 1, tile, frame, 1)
            s1[base : base + 8] = top
            s1[base + 56 : base + 64] = bottom
            s1[base + 48 : base + 56] = jnp.where(
                sub < 3, s1[base + 48 : base + 56], jnp.where(sub < 5, pltpu.roll(top, 4, 0), pltpu.roll(bottom, 6, 0))
            )
            s1[pl.ds(base, 8, stride=8)] = part(v, 0, tile, frame, 0)
            s1[pl.ds(base + 7, 8, stride=8)] = part(v, 0, tile, frame, 1)
            rows, chans = slice(frame * 64, frame * 64 + 64), slice(tile * 128, tile * 128 + 128)
            hid[rows, chans] = (s1[base : base + 64] * gate[rows, chans]).astype(BF16)

    for copy in halo:
        copy.wait_send()
    for step in range(1, 16):
        dest = lax.rem(me + step, 16)
        forward(dest).wait_send()
        back(dest).wait_send()


def body(latents, spatial_taps, kernel_taps, skip_gain, gate_weight, value_weight, out_weight):
    dma = pltpu.SemaphoreType.DMA
    hidden = pl.pallas_call(
        kernel,
        out_shape=jax.ShapeDtypeStruct((256, 512), BF16),
        in_specs=[pl.BlockSpec(memory_space=pl.ANY)] * 6,
        out_specs=pl.BlockSpec(memory_space=pltpu.VMEM),
        scratch_shapes=[
            pltpu.VMEM((4, 8, 8, 512), BF16),
            pltpu.VMEM((3, 3, 512), F32),
            pltpu.VMEM((64, 128), BF16),
            pltpu.VMEM((64, 128), F32),
            pltpu.VMEM((72, 8, 128), F32),
            pltpu.VMEM((1, 128), F32),
            pltpu.VMEM((512, 512), BF16),
            pltpu.VMEM((512, 512), BF16),
            pltpu.VMEM((1024, 128), F32),
            pltpu.VMEM((1024, 128), F32),
            pltpu.VMEM((2, 128, 128), BF16),
            pltpu.VMEM((4, 16, 128), BF16),
            pltpu.VMEM((2, 4, 8, 512), BF16),
            pltpu.VMEM((2, 128, 128), BF16),
            pltpu.VMEM((4, 16, 128), BF16),
            pltpu.VMEM((4, 16, 128), F32),
            pltpu.VMEM((2, 128, 128), F32),
            pltpu.VMEM((16, 4, 16, 128), BF16),
            pltpu.VMEM((16, 4, 16, 128), BF16),
            pltpu.VMEM((16, 4, 16, 128), BF16),
            pltpu.VMEM((16, 4, 16, 128), BF16),
            pltpu.VMEM((256, 512), F32),
            dma((6,)), dma((8,)), dma((8,)), dma((16,)), dma((16,)), dma((16,)), dma((16,)),
        ],
        compiler_params=pltpu.CompilerParams(
            collective_id=0, has_side_effects=True, vmem_limit_bytes=60 * 1024 * 1024
        ),
        name="mixing",
    )(latents, spatial_taps, kernel_taps, skip_gain.reshape(1, -1), gate_weight, value_weight)
    result = jnp.dot(hidden, out_weight, preferred_element_type=F32).astype(BF16)
    return result.reshape(latents.shape)


def solution(mesh):
    in_specs = (P("tm", "height", "width", None), P(), P(), P(), P(), P(), P())
    out_specs = P("tm", "height", "width", None)
    return jax.shard_map(body, mesh=mesh, in_specs=in_specs, out_specs=out_specs, check_vma=False)
```

time: 102 us -> 36.9 us (0.36); the launches traced: 100 us -> 36.8 us
  local copies, waits for them, and re-layouts: 49.5 us -> 0.01 us
  Pallas kernels: 0 us -> 34.8 us
  starting transfers between devices: 28.1 us -> 0 us
  waiting for transfers between devices: 17.2 us -> 0 us
  other arithmetic: 2.15 us -> 0 us
  matrix products: 3.13 us -> 1.96 us
    pallas_call x0 -> x1, Pallas kernels: none -> 34.8 us  [body(): pl.pallas_call(kernel, out_shape=jax.ShapeDtypeStruct((256, 512), BF16),...]
    all_to_all x2 -> x0, starting transfers between devices: 17.6 us -> none  [the longest x1 10.4 us: body(): lax.all_to_all(spatial, 'tm', split_axis=3, concat_axis=0, tiled=True)]
    unnamed x12 -> x2, local copies, waits for them, and re-layouts: 15.6 us -> 0.01 us
    gather x2 -> x0, local copies, waits for them, and re-layouts: 13.1 us -> none  [body(): picked = jnp.take(local_taps.T, index, axis=1)]
    all_to_all x2 -> x0, waiting for transfers between devices: 11.4 us -> none  [the longest x1 11.4 us: body(): lax.all_to_all(result.reshape(block.shape), 'tm', split_axis=0, concat_ax...]
    ppermute x4 -> x0, starting transfers between devices: 10.5 us -> none  [the longest x2 7.93 us: with_halo(): lax.ppermute(tail, axis, [(i, (i + 1) % count) for i in range(ends)])]
    all_to_all x2 -> x0, local copies, waits for them, and re-layouts: 6.56 us -> none  [the longest x1 5.34 us: body(): lax.all_to_all(spatial, 'tm', split_axis=3, concat_axis=0, tiled=True)]
    convert_element_type x1 -> x0, local copies, waits for them, and re-layouts: 6.37 us -> none  [spatial_mix(): return total.astype(jnp.bfloat16)]
  transfers between devices with their start and end apart: 6 -> 0, of which waited for: 3 -> 0; matrix products, arithmetic and copies ran while one was open for 17% -> 0% of each run, Pallas kernels for 0% -> 0%
where the time goes in v1:
time: 36.9 us; the launch traced here: 36.8 us
  Pallas kernels  34.8 us (94%)
  matrix products  1.96 us (5%)
    pallas_call x1, Pallas kernels, body(): pl.pallas_call(kernel, out_shape=jax.ShapeDtypeStruct((256, 512), BF16),...  34.8 us
    dot_general x1, matrix products, body(): jnp.dot(hidden, out_weight, preferred_element_type=F32).astype(BF16)  1.96 us

profile of v1, /device:TPU:1, one launch (start us, length us, event | category | flops | bytes accessed | tf_op | source)
XLA Modules:
  0.0 36.8 jit_solution(13643095661223847190)
XLA Ops:
  0.0 0.0 copy-start
  0.0 34.8 %mixing.1 = bf16[256,512]{1,0:T(8,128)(2,1)} custom-call(bf16[4,8,8,512]{3,2,1,0:T(8,128)(2,1)} %lat.1, f32[3,3,512]{2,1,0:T(4,128)} %taps.1, bf16[64,512]{1,0:T(8,128)(2,1)} %ktaps.1, f32[1,512]{1,0:T(1,128)} %bitcast.4, bf16[512,512]{1,0:T(8,128)(2,1)} %wg.1, bf16[512,512]{1,0:T(8,128)(2,1)} %wv.1), custom_call_target="tpu_custom_call" | custom-call | tf_op jit(solution)/shard_map/mixing/pallas_call | solution.py:330
  34.8 0.0 copy-done
  34.8 2.0 %convolution_convert_fusion = bf16[256,512]{1,0:T(8,128)(2,1)} fusion(bf16[256,512]{1,0:T(8,128)(2,1)} %mixing.1, bf16[512,512]{1,0:T(8,128)(2,1)S(1)} %copy-done), kind=kOutput, calls=%fused_computation | convolution fusion | flops 134348800 | bytes 1048576 | tf_op jit(solution)/shard_map/dot_general | solution.py:365
Async XLA Ops:
  0.0 34.8 %copy-start = (bf16[512,512]{1,0:T(8,128)(2,1)S(1)}, bf16[512,512]{1,0:T(8,128)(2,1)}, u32[]{:S(2)}) copy-start(bf16[512,512]{1,0:T(8,128)(2,1)} %param.13) | copy-start | bytes 1572868

commit v2 on v1

--- a/solution.py
+++ b/solution.py
@@ -49,11 +49,18 @@
         dh, dw = step
         return (me, lax.rem(hi + dh + nh, nh), lax.rem(wi + dw + nw, nw))
 
+    up, down, left, right = hi > 0, hi < nh - 1, wi > 0, wi < nw - 1
+    there = (up, down, left, right, up & left, up & right, down & left, down & right)
+    count = lambda flag: flag.astype(jnp.int32)
+    beside_count = (1 + count(up) + count(down)) * (1 + count(left) + count(right)) - 1
+
     barrier = pltpu.get_barrier_semaphore()
     for step in range(1, 16):
         pl.semaphore_signal(barrier, inc=1, device_id=peer(lax.rem(me + step, 16)), device_id_type=MESH)
-    for step in AROUND:
-        pl.semaphore_signal(barrier, inc=1, device_id=beside(step), device_id_type=MESH)
+    for step, has in zip(AROUND, there):
+        @pl.when(has)
+        def _():
+            pl.semaphore_signal(barrier, inc=1, device_id=beside(step), device_id_type=MESH)
     for load in loads[2:]:
         load.start()
 
@@ -67,7 +74,13 @@
     for n, site in enumerate((0, 7, 56, 63)):
         crnb[n] = s0[pl.ds(site, 16, stride=64)].astype(BF16)
 
-    pl.semaphore_wait(barrier, 23)
+    slots = (hrow.at[0], hrow.at[1], hcol.at[0], hcol.at[1], hcrn.at[0], hcrn.at[1], hcrn.at[2], hcrn.at[3])
+    for slot, has in zip(slots, there):
+        @pl.when(jnp.logical_not(has))
+        def _():
+            slot[...] = jnp.zeros(slot.shape, BF16)
+
+    pl.semaphore_wait(barrier, 15 + beside_count)
 
     pieces = (
         (xl.at[:, 0], hrow.at[1]),
@@ -88,8 +101,8 @@
                 device_id=beside(AROUND[n]), device_id_type=MESH,
             )
         )
-    for copy in halo:
-        copy.start()
+    for copy, has in zip(halo, there):
+        pl.when(has)(copy.start)
 
     sub = lax.broadcasted_iota(jnp.int32, (8, 128), 0)
     first, last = sub == 0, sub == 7
@@ -161,29 +174,21 @@
     spread(0)
 
     for n, (src, dst) in enumerate(pieces):
-        pltpu.make_async_remote_copy(
-            src_ref=src, dst_ref=(hrow.at[0], hrow.at[1], hcol.at[0], hcol.at[1], hcrn.at[0], hcrn.at[1], hcrn.at[2], hcrn.at[3])[n],
-            send_sem=hs.at[n], recv_sem=hr.at[n], device_id=beside(AROUND[n]), device_id_type=MESH,
-        ).wait_recv()
-
-    up = (hi > 0).astype(F32)
-    down = (hi < nh - 1).astype(F32)
-    left = (wi > 0).astype(F32)
-    right = (wi < nw - 1).astype(F32)
-    hk32[0] = hcol[0].astype(F32) * left
-    hk32[1] = hcol[1].astype(F32) * right
-    hc32[0] = hcrn[0].astype(F32) * (up * left)
-    hc32[1] = hcrn[1].astype(F32) * (up * right)
-    hc32[2] = hcrn[2].astype(F32) * (down * left)
-    hc32[3] = hcrn[3].astype(F32) * (down * right)
+        copy = pltpu.make_async_remote_copy(
+            src_ref=src, dst_ref=slots[n], send_sem=hs.at[n], recv_sem=hr.at[n],
+            device_id=beside(AROUND[n]), device_id_type=MESH,
+        )
+        pl.when(there[n])(copy.wait_recv)
+    hk32[...] = hcol[...].astype(F32)
+    hc32[...] = hcrn[...].astype(F32)
 
     def border(i, carry):
         tile, frame = i // 4, lax.rem(i, 4)
         base = pl.multiple_of(i * 64, 64)
         chans = pl.ds(pl.multiple_of(tile * 128, 128), 128)
         weights = [[tap(tile, a, b) for b in range(3)] for a in range(3)]
-        above = hrow[0, frame, :, chans].astype(F32) * up
-        below = hrow[1, frame, :, chans].astype(F32) * down
+        above = hrow[0, frame, :, chans].astype(F32)
+        below = hrow[1, frame, :, chans].astype(F32)
         row0 = s1[pl.ds(base, 8)] + (weights[0][0] * west(above) + weights[0][1] * above + weights[0][2] * east(above))
         row7 = s1[pl.ds(base + 56, 8)] + (weights[2][0] * west(below) + weights[2][1] * below + weights[2][2] * east(below))
         row6 = s1[pl.ds(base + 48, 8)]
@@ -317,8 +322,8 @@
             rows, chans = slice(frame * 64, frame * 64 + 64), slice(tile * 128, tile * 128 + 128)
             hid[rows, chans] = (s1[base : base + 64] * gate[rows, chans]).astype(BF16)
 
-    for copy in halo:
-        copy.wait_send()
+    for copy, has in zip(halo, there):
+        pl.when(has)(copy.wait_send)
     for step in range(1, 16):
         dest = lax.rem(me + step, 16)
         forward(dest).wait_send()
@@ -329,7 +334,7 @@
     dma = pltpu.SemaphoreType.DMA
     hidden = pl.pallas_call(
         kernel,
-        out_shape=jax.ShapeDtypeStruct((256, 512), BF16),
+        out_shape=pltpu.VMEM((256, 512), BF16),
         in_specs=[pl.BlockSpec(memory_space=pl.ANY)] * 6,
         out_specs=pl.BlockSpec(memory_space=pltpu.VMEM),
         scratch_shapes=[

time: 36.9 us -> 29 us (0.79)
  Pallas kernels: 34.8 us -> 27.8 us
  matrix products: 1.96 us -> 1.01 us
    pallas_call x1, Pallas kernels: 34.8 us -> 27.8 us  [body(): pl.pallas_call(kernel, out_shape=pltpu.VMEM((256, 512), BF16), in_specs=[...]
    dot_general x1, matrix products: 1.96 us -> 1.01 us  [body(): jnp.dot(hidden, out_weight, preferred_element_type=F32).astype(BF16)]
where the time goes in v2:
time: 29 us; the launch traced here: 28.8 us
  Pallas kernels  27.8 us (96%)
  matrix products  1.01 us (3%)
    pallas_call x1, Pallas kernels, body(): pl.pallas_call(kernel, out_shape=pltpu.VMEM((256, 512), BF16), in_specs=[...  27.8 us
    dot_general x1, matrix products, body(): jnp.dot(hidden, out_weight, preferred_element_type=F32).astype(BF16)  1.01 us

profile of v2, /device:TPU:1, one launch (start us, length us, event | category | flops | bytes accessed | tf_op | source)
XLA Modules:
  0.0 28.8 jit_solution(3305456072511201720)
XLA Ops:
  0.0 0.0 copy-start
  0.0 27.8 %mixing.1 = bf16[256,512]{1,0:T(8,128)(2,1)S(1)} custom-call(bf16[4,8,8,512]{3,2,1,0:T(8,128)(2,1)} %lat.1, f32[3,3,512]{2,1,0:T(4,128)} %taps.1, bf16[64,512]{1,0:T(8,128)(2,1)} %ktaps.1, f32[1,512]{1,0:T(1,128)} %bitcast.4, bf16[512,512]{1,0:T(8,128)(2,1)} %wg.1, bf16[512,512]{1,0:T(8,128)(2,1)} %wv.1), custom_call_target="tpu_custom_call" | custom-call | tf_op jit(solution)/shard_map/mixing/pallas_call | solution.py:335
  27.8 0.0 copy-done
  27.8 1.0 %convolution_convert_fusion = bf16[256,512]{1,0:T(8,128)(2,1)} fusion(bf16[256,512]{1,0:T(8,128)(2,1)S(1)} %mixing.1, bf16[512,512]{1,0:T(8,128)(2,1)S(1)} %copy-done), kind=kOutput, calls=%fused_computation | convolution fusion | flops 134348800 | bytes 1048576 | tf_op jit(solution)/shard_map/dot_general | solution.py:370
Async XLA Ops:
  0.0 27.8 %copy-start = (bf16[512,512]{1,0:T(8,128)(2,1)S(1)}, bf16[512,512]{1,0:T(8,128)(2,1)}, u32[]{:S(2)}) copy-start(bf16[512,512]{1,0:T(8,128)(2,1)} %param.13) | copy-start | bytes 1572868

commit v3 on v2

--- a/solution.py
+++ b/solution.py
@@ -10,7 +10,7 @@
 MESH = pl.DeviceIdType.MESH
 F32 = jnp.float32
 BF16 = jnp.bfloat16
-ORDER = (1, 7, 2, 6, 3, 5, 4, 0)
+ORDER = (4, 3, 5, 2, 6, 1, 7, 0)
 AROUND = ((-1, 0), (1, 0), (0, -1), (0, 1), (-1, -1), (-1, 1), (1, -1), (1, 1))
 
 
@@ -55,7 +55,7 @@
     beside_count = (1 + count(up) + count(down)) * (1 + count(left) + count(right)) - 1
 
     barrier = pltpu.get_barrier_semaphore()
-    for step in range(1, 16):
+    for step in (8, 9, 7, 10, 6, 11, 5, 12, 4, 13, 3, 14, 2, 15, 1):
         pl.semaphore_signal(barrier, inc=1, device_id=peer(lax.rem(me + step, 16)), device_id_type=MESH)
     for step, has in zip(AROUND, there):
         @pl.when(has)
@@ -79,30 +79,6 @@
         @pl.when(jnp.logical_not(has))
         def _():
             slot[...] = jnp.zeros(slot.shape, BF16)
-
-    pl.semaphore_wait(barrier, 15 + beside_count)
-
-    pieces = (
-        (xl.at[:, 0], hrow.at[1]),
-        (xl.at[:, 7], hrow.at[0]),
-        (colb.at[0], hcol.at[1]),
-        (colb.at[1], hcol.at[0]),
-        (crnb.at[0], hcrn.at[3]),
-        (crnb.at[1], hcrn.at[2]),
-        (crnb.at[2], hcrn.at[1]),
-        (crnb.at[3], hcrn.at[0]),
-    )
-    opposite = (1, 0, 3, 2, 7, 6, 5, 4)
-    halo = []
-    for n, (src, dst) in enumerate(pieces):
-        halo.append(
-            pltpu.make_async_remote_copy(
-                src_ref=src, dst_ref=dst, send_sem=hs.at[n], recv_sem=hr.at[opposite[n]],
-                device_id=beside(AROUND[n]), device_id_type=MESH,
-            )
-        )
-    for copy, has in zip(halo, there):
-        pl.when(has)(copy.start)
 
     sub = lax.broadcasted_iota(jnp.int32, (8, 128), 0)
     first, last = sub == 0, sub == 7
@@ -147,6 +123,30 @@
         return carry
 
     lax.fori_loop(0, 16, inside, 0)
+
+    pl.semaphore_wait(barrier, 15 + beside_count)
+
+    pieces = (
+        (xl.at[:, 0], hrow.at[1]),
+        (xl.at[:, 7], hrow.at[0]),
+        (colb.at[0], hcol.at[1]),
+        (colb.at[1], hcol.at[0]),
+        (crnb.at[0], hcrn.at[3]),
+        (crnb.at[1], hcrn.at[2]),
+        (crnb.at[2], hcrn.at[1]),
+        (crnb.at[3], hcrn.at[0]),
+    )
+    opposite = (1, 0, 3, 2, 7, 6, 5, 4)
+    halo = []
+    for n, (src, dst) in enumerate(pieces):
+        halo.append(
+            pltpu.make_async_remote_copy(
+                src_ref=src, dst_ref=dst, send_sem=hs.at[n], recv_sem=hr.at[opposite[n]],
+                device_id=beside(AROUND[n]), device_id_type=MESH,
+            )
+        )
+    for copy, has in zip(halo, there):
+        pl.when(has)(copy.start)
 
     def forward(dest):
         return pltpu.make_async_remote_copy(

time: 29 us -> 27.3 us (0.941)
  Pallas kernels: 27.8 us -> 26.1 us
    pallas_call x1, Pallas kernels: 27.8 us -> 26.1 us  [body(): pl.pallas_call(kernel, out_shape=pltpu.VMEM((256, 512), BF16), in_specs=[...]
where the time goes in v3:
time: 27.3 us; the launch traced here: 27.1 us
  Pallas kernels  26.1 us (96%)
  matrix products  1.01 us (4%)
    pallas_call x1, Pallas kernels, body(): pl.pallas_call(kernel, out_shape=pltpu.VMEM((256, 512), BF16), in_specs=[...  26.1 us
    dot_general x1, matrix products, body(): jnp.dot(hidden, out_weight, preferred_element_type=F32).astype(BF16)  1.01 us

profile of v3, /device:TPU:1, one launch (start us, length us, event | category | flops | bytes accessed | tf_op | source)
XLA Modules:
  0.0 27.1 jit_solution(3778133176441945166)
XLA Ops:
  0.0 0.0 copy-start
  0.0 26.1 %mixing.1 = bf16[256,512]{1,0:T(8,128)(2,1)S(1)} custom-call(bf16[4,8,8,512]{3,2,1,0:T(8,128)(2,1)} %lat.1, f32[3,3,512]{2,1,0:T(4,128)} %taps.1, bf16[64,512]{1,0:T(8,128)(2,1)} %ktaps.1, f32[1,512]{1,0:T(1,128)} %bitcast.4, bf16[512,512]{1,0:T(8,128)(2,1)} %wg.1, bf16[512,512]{1,0:T(8,128)(2,1)} %wv.1), custom_call_target="tpu_custom_call" | custom-call | tf_op jit(solution)/shard_map/mixing/pallas_call | solution.py:335
  26.1 0.0 copy-done
  26.1 1.0 %convolution_convert_fusion = bf16[256,512]{1,0:T(8,128)(2,1)} fusion(bf16[256,512]{1,0:T(8,128)(2,1)S(1)} %mixing.1, bf16[512,512]{1,0:T(8,128)(2,1)S(1)} %copy-done), kind=kOutput, calls=%fused_computation | convolution fusion | flops 134348800 | bytes 1048576 | tf_op jit(solution)/shard_map/dot_general | solution.py:370
Async XLA Ops:
  0.0 26.1 %copy-start = (bf16[512,512]{1,0:T(8,128)(2,1)S(1)}, bf16[512,512]{1,0:T(8,128)(2,1)}, u32[]{:S(2)}) copy-start(bf16[512,512]{1,0:T(8,128)(2,1)} %param.13) | copy-start | bytes 1572868

commit v4 on v3

--- a/solution.py
+++ b/solution.py
@@ -157,21 +157,21 @@
     def keep():
         return pltpu.make_async_copy(sendb.at[me], xin.at[me], fr.at[me])
 
-    def spread(which):
-        for step in ORDER:
-            dest = lax.rem(ring + step, 8) * 2 + which
-            if step:
+    def spread(which, turn=None):
+        for near, far in zip((4, 2, 6, 0), (3, 5, 1, 7)):
+            odd = lax.rem(ring + turn, 2)
+            dest = lax.rem(ring + near + odd * (far - near), 8) * 2 + which
+
+            @pl.when(dest == me)
+            def _():
+                keep().start()
+
+            @pl.when(dest != me)
+            def _():
                 forward(dest).start()
-            else:
-                @pl.when(core == which)
-                def _():
-                    keep().start()
-
-                @pl.when(core != which)
-                def _():
-                    forward(dest).start()
-
-    spread(0)
+
+    spread(0, 0)
+    spread(0, 1)
 
     for n, (src, dst) in enumerate(pieces):
         copy = pltpu.make_async_remote_copy(
@@ -211,7 +211,8 @@
         return carry
 
     lax.fori_loop(0, 16, border, 0)
-    spread(1)
+    spread(1, 0)
+    spread(1, 1)
 
     loads[2].wait()
     loads[3].wait()
@@ -246,7 +247,7 @@
     def own():
         return pltpu.make_async_copy(retb.at[me], mixin.at[me], rr.at[me])
 
-    for step in ORDER:
+    for step in (3, 5, 4, 2, 6, 1, 7, 0):
         chip = lax.rem(ring + step, 8)
 
         def lagged(source, acc):

time: 27.3 us -> 26.7 us (0.978)
  Pallas kernels: 26.1 us -> 25.6 us
    pallas_call x1, Pallas kernels: 26.1 us -> 25.6 us  [body(): pl.pallas_call(kernel, out_shape=pltpu.VMEM((256, 512), BF16), in_specs=[...]
where the time goes in v4:
time: 26.7 us; the launch traced here: 26.6 us
  Pallas kernels  25.6 us (96%)
  matrix products  1.01 us (4%)
    pallas_call x1, Pallas kernels, body(): pl.pallas_call(kernel, out_shape=pltpu.VMEM((256, 512), BF16), in_specs=[...  25.6 us
    dot_general x1, matrix products, body(): jnp.dot(hidden, out_weight, preferred_element_type=F32).astype(BF16)  1.01 us

profile of v4, /device:TPU:1, one launch (start us, length us, event | category | flops | bytes accessed | tf_op | source)
XLA Modules:
  0.0 26.6 jit_solution(8004456508407517874)
XLA Ops:
  0.0 0.0 copy-start
  0.0 25.6 %mixing.1 = bf16[256,512]{1,0:T(8,128)(2,1)S(1)} custom-call(bf16[4,8,8,512]{3,2,1,0:T(8,128)(2,1)} %lat.1, f32[3,3,512]{2,1,0:T(4,128)} %taps.1, bf16[64,512]{1,0:T(8,128)(2,1)} %ktaps.1, f32[1,512]{1,0:T(1,128)} %bitcast.4, bf16[512,512]{1,0:T(8,128)(2,1)} %wg.1, bf16[512,512]{1,0:T(8,128)(2,1)} %wv.1), custom_call_target="tpu_custom_call" | custom-call | tf_op jit(solution)/shard_map/mixing/pallas_call | solution.py:336
  25.6 0.0 copy-done
  25.6 1.0 %convolution_convert_fusion = bf16[256,512]{1,0:T(8,128)(2,1)} fusion(bf16[256,512]{1,0:T(8,128)(2,1)S(1)} %mixing.1, bf16[512,512]{1,0:T(8,128)(2,1)S(1)} %copy-done), kind=kOutput, calls=%fused_computation | convolution fusion | flops 134348800 | bytes 1048576 | tf_op jit(solution)/shard_map/dot_general | solution.py:371
Async XLA Ops:
  0.0 25.6 %copy-start = (bf16[512,512]{1,0:T(8,128)(2,1)S(1)}, bf16[512,512]{1,0:T(8,128)(2,1)}, u32[]{:S(2)}) copy-start(bf16[512,512]{1,0:T(8,128)(2,1)} %param.13) | copy-start | bytes 1572868

commit v5 on v4

--- a/solution.py
+++ b/solution.py
@@ -230,13 +230,13 @@
     gate[...] = raw / (1.0 + jnp.exp(-raw))
     loads[5].wait()
 
-    keep().wait()
-    for step in range(1, 16):
-        src = lax.rem(me + step, 16)
-        pltpu.make_async_remote_copy(
+    def filtered(src):
+        copy = pltpu.make_async_remote_copy(
             src_ref=sendb.at[src], dst_ref=xin.at[src], send_sem=fs.at[src], recv_sem=fr.at[src],
             device_id=peer(src), device_id_type=MESH,
-        ).wait_recv()
+        )
+        pl.when(src == me)(lambda: keep().wait())
+        pl.when(src != me)(copy.wait_recv)
 
     def back(dest):
         return pltpu.make_async_remote_copy(
@@ -247,8 +247,11 @@
     def own():
         return pltpu.make_async_copy(retb.at[me], mixin.at[me], rr.at[me])
 
-    for step in (3, 5, 4, 2, 6, 1, 7, 0):
-        chip = lax.rem(ring + step, 8)
+    turn = lax.rem(ring + 4, 6)
+    for turn_no, chip in enumerate([0, 1] + [2 + lax.rem(turn + step, 6) for step in (3, 2, 4, 1, 5, 0)]):
+        if turn_no in (0, 2):
+            for src in range(4) if turn_no == 0 else range(4, 16):
+                filtered(src)
 
         def lagged(source, acc):
             shift = 8 + 8 * (chip - source)
@@ -259,12 +262,9 @@
 
         acc = lax.fori_loop(0, chip + 1, lagged, jnp.zeros((8, 2, 8, 128), F32))
         retb[pl.ds(chip * 2, 2)] = acc.reshape(2, 4, 16, 128).astype(BF16)
-        if step:
-            back(chip * 2).start()
-            back(chip * 2 + 1).start()
-        else:
-            own().start()
-            back(chip * 2 + 1 - core).start()
+        for dest in (chip * 2, chip * 2 + 1):
+            pl.when(dest == me)(lambda: own().start())
+            pl.when(dest != me)(back(dest).start)
 
     def arrived(which):
         for step in ORDER:

time: 26.7 us -> 26.2 us (0.981)
  the two profiles are of different devices: /device:TPU:1 before, /device:TPU:209 now
where the time goes in v5:
time: 26.2 us; the launch traced here: 26.1 us
  Pallas kernels  25.1 us (96%)
  matrix products  1.01 us (4%)
    pallas_call x1, Pallas kernels, body(): pl.pallas_call(kernel, out_shape=pltpu.VMEM((256, 512), BF16), in_specs=[...  25.1 us
    dot_general x1, matrix products, body(): jnp.dot(hidden, out_weight, preferred_element_type=F32).astype(BF16)  1.01 us

profile of v5, /device:TPU:209, one launch (start us, length us, event | category | flops | bytes accessed | tf_op | source)
XLA Modules:
  0.0 26.1 jit_solution(11918464414291291000)
XLA Ops:
  0.0 0.0 copy-start
  0.0 25.1 %mixing.1 = bf16[256,512]{1,0:T(8,128)(2,1)S(1)} custom-call(bf16[4,8,8,512]{3,2,1,0:T(8,128)(2,1)} %lat.1, f32[3,3,512]{2,1,0:T(4,128)} %taps.1, bf16[64,512]{1,0:T(8,128)(2,1)} %ktaps.1, f32[1,512]{1,0:T(1,128)} %bitcast.4, bf16[512,512]{1,0:T(8,128)(2,1)} %wg.1, bf16[512,512]{1,0:T(8,128)(2,1)} %wv.1), custom_call_target="tpu_custom_call" | custom-call | tf_op jit(solution)/shard_map/mixing/pallas_call | solution.py:336
  25.1 0.0 copy-done
  25.1 1.0 %convolution_convert_fusion = bf16[256,512]{1,0:T(8,128)(2,1)} fusion(bf16[256,512]{1,0:T(8,128)(2,1)S(1)} %mixing.1, bf16[512,512]{1,0:T(8,128)(2,1)S(1)} %copy-done), kind=kOutput, calls=%fused_computation | convolution fusion | flops 134348800 | bytes 1048576 | tf_op jit(solution)/shard_map/dot_general | solution.py:371
Async XLA Ops:
  0.0 25.1 %copy-start = (bf16[512,512]{1,0:T(8,128)(2,1)S(1)}, bf16[512,512]{1,0:T(8,128)(2,1)}, u32[]{:S(2)}) copy-start(bf16[512,512]{1,0:T(8,128)(2,1)} %param.13) | copy-start | bytes 1572868

commit v6 on v5

--- a/solution.py
+++ b/solution.py
@@ -157,10 +157,14 @@
     def keep():
         return pltpu.make_async_copy(sendb.at[me], xin.at[me], fr.at[me])
 
-    def spread(which, turn=None):
-        for near, far in zip((4, 2, 6, 0), (3, 5, 1, 7)):
-            odd = lax.rem(ring + turn, 2)
-            dest = lax.rem(ring + near + odd * (far - near), 8) * 2 + which
+    def spread(which):
+        chips = []
+        for step in range(4):
+            chip = step
+            apart = lax.rem(ring - chip + 8, 8)
+            near = 4 * ((apart < 2) | (apart > 6)).astype(jnp.int32)
+            chips += [chip + near, chip + 4 - near]
+        for dest in [chip * 2 + which for chip in chips]:
 
             @pl.when(dest == me)
             def _():
@@ -170,8 +174,7 @@
             def _():
                 forward(dest).start()
 
-    spread(0, 0)
-    spread(0, 1)
+    spread(0)
 
     for n, (src, dst) in enumerate(pieces):
         copy = pltpu.make_async_remote_copy(
@@ -211,8 +214,7 @@
         return carry
 
     lax.fori_loop(0, 16, border, 0)
-    spread(1, 0)
-    spread(1, 1)
+    spread(1)
 
     loads[2].wait()
     loads[3].wait()

time: 26.2 us -> 26.5 us (1.011)
  the two profiles are of different devices: /device:TPU:209 before, /device:TPU:211 now
where the time goes in v6:
time: 26.5 us; the launch traced here: 26.4 us
  Pallas kernels  25.3 us (95%)
  matrix products  1.01 us (4%)
    pallas_call x1, Pallas kernels, body(): pl.pallas_call(kernel, out_shape=pltpu.VMEM((256, 512), BF16), in_specs=[...  25.3 us
    dot_general x1, matrix products, body(): jnp.dot(hidden, out_weight, preferred_element_type=F32).astype(BF16)  1.01 us

profile of v6, /device:TPU:211, one launch (start us, length us, event | category | flops | bytes accessed | tf_op | source)
XLA Modules:
  0.0 26.4 jit_solution(4328268520678316692)
XLA Ops:
  0.0 0.0 copy-start
  0.0 25.3 %mixing.1 = bf16[256,512]{1,0:T(8,128)(2,1)S(1)} custom-call(bf16[4,8,8,512]{3,2,1,0:T(8,128)(2,1)} %lat.1, f32[3,3,512]{2,1,0:T(4,128)} %taps.1, bf16[64,512]{1,0:T(8,128)(2,1)} %ktaps.1, f32[1,512]{1,0:T(1,128)} %bitcast.4, bf16[512,512]{1,0:T(8,128)(2,1)} %wg.1, bf16[512,512]{1,0:T(8,128)(2,1)} %wv.1), custom_call_target="tpu_custom_call" | custom-call | tf_op jit(solution)/shard_map/mixing/pallas_call | solution.py:338
  25.4 0.0 copy-done
  25.4 1.0 %convolution_convert_fusion = bf16[256,512]{1,0:T(8,128)(2,1)} fusion(bf16[256,512]{1,0:T(8,128)(2,1)S(1)} %mixing.1, bf16[512,512]{1,0:T(8,128)(2,1)S(1)} %copy-done), kind=kOutput, calls=%fused_computation | convolution fusion | flops 134348800 | bytes 1048576 | tf_op jit(solution)/shard_map/dot_general | solution.py:373
Async XLA Ops:
  0.0 25.4 %copy-start = (bf16[512,512]{1,0:T(8,128)(2,1)S(1)}, bf16[512,512]{1,0:T(8,128)(2,1)}, u32[]{:S(2)}) copy-start(bf16[512,512]{1,0:T(8,128)(2,1)} %param.13) | copy-start | bytes 1572868

commit v7 on v5

--- a/solution.py
+++ b/solution.py
@@ -248,7 +248,7 @@
         return pltpu.make_async_copy(retb.at[me], mixin.at[me], rr.at[me])
 
     turn = lax.rem(ring + 4, 6)
-    for turn_no, chip in enumerate([0, 1] + [2 + lax.rem(turn + step, 6) for step in (3, 2, 4, 1, 5, 0)]):
+    for turn_no, chip in enumerate([0, 1] + [2 + lax.rem(turn + step, 6) for step in (2, 4, 3, 1, 5, 0)]):
         if turn_no in (0, 2):
             for src in range(4) if turn_no == 0 else range(4, 16):
                 filtered(src)

time: 26.2 us -> 26.5 us (1.011)
  the two profiles are of different devices: /device:TPU:209 before, /device:TPU:193 now
where the time goes in v7:
time: 26.5 us; the launch traced here: 26.4 us
  Pallas kernels  25.4 us (96%)
  matrix products  1.01 us (4%)
    pallas_call x1, Pallas kernels, body(): pl.pallas_call(kernel, out_shape=pltpu.VMEM((256, 512), BF16), in_specs=[...  25.4 us
    dot_general x1, matrix products, body(): jnp.dot(hidden, out_weight, preferred_element_type=F32).astype(BF16)  1.01 us

profile of v7, /device:TPU:193, one launch (start us, length us, event | category | flops | bytes accessed | tf_op | source)
XLA Modules:
  0.0 26.4 jit_solution(8116899630801859085)
XLA Ops:
  0.0 0.0 copy-start
  0.0 25.4 %mixing.1 = bf16[256,512]{1,0:T(8,128)(2,1)S(1)} custom-call(bf16[4,8,8,512]{3,2,1,0:T(8,128)(2,1)} %lat.1, f32[3,3,512]{2,1,0:T(4,128)} %taps.1, bf16[64,512]{1,0:T(8,128)(2,1)} %ktaps.1, f32[1,512]{1,0:T(1,128)} %bitcast.4, bf16[512,512]{1,0:T(8,128)(2,1)} %wg.1, bf16[512,512]{1,0:T(8,128)(2,1)} %wv.1), custom_call_target="tpu_custom_call" | custom-call | tf_op jit(solution)/shard_map/mixing/pallas_call | solution.py:336
  25.4 0.0 copy-done
  25.4 1.0 %convolution_convert_fusion = bf16[256,512]{1,0:T(8,128)(2,1)} fusion(bf16[256,512]{1,0:T(8,128)(2,1)S(1)} %mixing.1, bf16[512,512]{1,0:T(8,128)(2,1)S(1)} %copy-done), kind=kOutput, calls=%fused_computation | convolution fusion | flops 134348800 | bytes 1048576 | tf_op jit(solution)/shard_map/dot_general | solution.py:371
Async XLA Ops:
  0.0 25.4 %copy-start = (bf16[512,512]{1,0:T(8,128)(2,1)S(1)}, bf16[512,512]{1,0:T(8,128)(2,1)}, u32[]{:S(2)}) copy-start(bf16[512,512]{1,0:T(8,128)(2,1)} %param.13) | copy-start | bytes 1572868
